TPU v7x, 32 devices: a whole 2x2x4 slice. The times are simulated.
32 devices in a mesh: seq: 16 (over z, y, x), head: 2 (over core).
Axes of the slice: x: 2, y: 2, z: 4, core: 2. Of those that a mesh axis runs over, the one named last changes fastest.
Arguments:
- q_lin: bfloat16 [4096, 512], P('seq', 'head'), may hold values from -6 to 6
- k_lin: bfloat16 [4096, 512], P('seq', 'head'), may hold values from -6 to 6
- v_lin: bfloat16 [4096, 512], P('seq', 'head'), may hold values from -6 to 6
- log_decay: float32 [4, 4096], P('head', 'seq'), may hold values from -0.4 to 0, as said below
- q_soft: bfloat16 [4096, 512], P('seq', 'head'), may hold values from -12 to 12
- k_soft: bfloat16 [4096, 512], P('seq', 'head'), may hold values from -6 to 6
- v_soft: bfloat16 [4096, 512], P('seq', 'head'), may hold values from -6 to 6
- wo_lin: bfloat16 [512, 4096], P('head'), may hold values from -0.375 to 0.375
- wo_soft: bfloat16 [512, 4096], P('head'), may hold values from -0.375 to 0.375
Outputs:
- lin_mixed: bfloat16 [4096, 4096], P('seq', 'head')
- soft_mixed: bfloat16 [4096, 4096], P('seq', 'head')
Inputs may be any that keep to these rules, and one draw needn't show every extreme that they name: `log_decay`: log decays are never positive.
All inputs are finite; a program needn't handle non-finite values.
Results may differ from a plain program's by a relative error of at most 0.012.
Values may be sent and summed in bfloat16 or wider, within the bound.
A program may use at most 64 MiB of HBM per device.

v0:
```python
import math
import jax
import jax.numpy as jnp
from jax import lax
from jax.sharding import PartitionSpec as P

HIGHEST = lax.Precision.HIGHEST
NEG_BIG = -1e30


def prefix(shard, axis, combine, identity):
    size, here = (lax.axis_size(axis), lax.axis_index(axis))
    everything = jax.tree.map(
        lambda part, kind: lax.all_gather(part.astype(kind), axis),
        shard,
        (jnp.bfloat16, jnp.bfloat16),
    )
    start = jax.tree.map(
        lambda part, zero: jnp.broadcast_to(jnp.asarray(zero, part.dtype), part.shape),
        shard,
        identity,
    )

    def turn(k, before):
        reached = k < here
        new = combine(
            before, jax.tree.map(lambda part, own: part[k].astype(own.dtype), everything, shard)
        )
        return jax.tree.map(lambda a, b: jnp.where(reached, a, b), new, before)

    return lax.fori_loop(0, size, turn, start)


def second_half(device):
    return 2 * device + 1


def absorb(state, query_half, key_block, value_block, allowed, factor):
    row_top, row_sum, weighted = state
    scores = (
        jnp.einsum("qhd,khd->hqk", query_half, key_block, preferred_element_type=jnp.float32)
        * factor
    )
    if allowed is not None:
        scores = jnp.where(allowed[None], scores, -jnp.inf)
    new_top = jnp.maximum(row_top, jnp.max(scores, axis=-1))
    shrink = jnp.exp(row_top - new_top)
    weights = jnp.exp(scores - new_top[:, :, None])
    row_sum = row_sum * shrink + jnp.sum(weights, axis=-1)
    weighted = weighted * shrink.T[:, :, None] + jnp.einsum(
        "hqk,khd->qhd",
        weights.astype(jnp.bfloat16),
        value_block,
        preferred_element_type=jnp.float32,
    )
    return (new_top, row_sum, weighted)


def lightning_heads(q_lin, k_lin, v_lin, log_decay):
    row_count = q_lin.shape[0]
    head_count = log_decay.shape[0]
    head_width = q_lin.shape[1] // head_count
    query_plain = q_lin.reshape(row_count, head_count, head_width)
    key_plain = k_lin.reshape(row_count, head_count, head_width)
    queries = query_plain.astype(jnp.float32)
    key_rows = key_plain.astype(jnp.float32)
    values = v_lin.astype(jnp.float32).reshape(row_count, head_count, head_width)
    cumulative = jnp.cumsum(log_decay, axis=1)
    lower = jnp.arange(row_count)[:, None] >= jnp.arange(row_count)[None, :]
    decay_gap = jnp.where(lower[None], cumulative[:, :, None] - cumulative[:, None, :], -jnp.inf)
    scores = jnp.einsum(
        "thd,shd->hts", query_plain, key_plain, preferred_element_type=jnp.float32
    ) * jnp.exp(decay_gap)
    inside = jnp.einsum("hts,shd->thd", scores, values, precision=HIGHEST)
    closing = jnp.exp(cumulative[:, -1:] - cumulative)
    own_state = jnp.einsum(
        "shd,she->hde", key_rows * closing.T[:, :, None], values, precision=HIGHEST
    )
    own_decay = cumulative[:, -1]

    def combine(earlier, later):
        return (jnp.exp(later[1])[:, None, None] * earlier[0] + later[0], earlier[1] + later[1])

    identity = (jnp.zeros_like(own_state), jnp.zeros_like(own_decay))
    carried, _ = prefix((own_state, own_decay), "seq", combine, identity)
    from_before = (
        jnp.einsum("thd,hde->the", queries, carried, precision=HIGHEST)
        * jnp.exp(cumulative).T[:, :, None]
    )
    raw = inside + from_before
    factor = lax.rsqrt(jnp.mean(raw * raw, axis=-1, keepdims=True) + 1e-06)
    return (raw * factor).astype(jnp.bfloat16).reshape(row_count, head_count * head_width)


def softmax_heads(q_soft, k_soft, v_soft, head_width):
    row_count = q_soft.shape[0]
    half_rows = row_count // 2
    head_count = q_soft.shape[1] // head_width
    own_index = lax.axis_index("seq")
    factor = 1.0 / math.sqrt(head_width)
    shaped = q_soft.reshape(2, half_rows, head_count, head_width)
    query_ids = (2 * own_index, second_half(own_index))
    triangle = jnp.arange(half_rows)[:, None] >= jnp.arange(half_rows)[None, :]

    def block_pass(state, side, key_block, value_block, key_id):

        def full_block(inner_state):
            return absorb(inner_state, shaped[side], key_block, value_block, None, factor)

        def diagonal_block(inner_state):
            return absorb(inner_state, shaped[side], key_block, value_block, triangle, factor)

        def skipped(inner_state):
            return inner_state

        def not_below(inner_state):
            return lax.cond(key_id == query_ids[side], diagonal_block, skipped, inner_state)

        return lax.cond(key_id < query_ids[side], full_block, not_below, state)

    start_state = tuple(
        (
            (
                jnp.full((head_count, half_rows), NEG_BIG, jnp.float32),
                jnp.zeros((head_count, half_rows), jnp.float32),
                jnp.zeros((half_rows, head_count, head_width), jnp.float32),
            )
            for side in range(2)
        )
    )
    carry = start_state
    key_piece = lax.all_gather(k_soft, "seq", axis=0, tiled=True)
    value_piece = lax.all_gather(v_soft, "seq", axis=0, tiled=True)
    piece_rows = key_piece.shape[0]
    blocks = piece_rows // half_rows
    key_blocks = key_piece.reshape(blocks, half_rows, head_count, head_width)
    value_blocks = value_piece.reshape(blocks, half_rows, head_count, head_width)
    firsts = half_rows * jnp.arange(blocks, dtype=jnp.int32)

    def inner(state, block_item):
        key_block, value_block, first = block_item
        key_id = first // half_rows
        return (
            tuple(
                (block_pass(state[side], side, key_block, value_block, key_id) for side in range(2))
            ),
            None,
        )

    carry, _ = lax.scan(inner, carry, (key_blocks, value_blocks, firsts))
    halves = [
        (carry[side][2] / carry[side][1].T[:, :, None])
        .astype(jnp.bfloat16)
        .reshape(half_rows, head_count * head_width)
        for side in range(2)
    ]
    return jnp.concatenate(halves, axis=0)


def local(q_lin, k_lin, v_lin, log_decay, q_soft, k_soft, v_soft, wo_lin, wo_soft):
    head_width = q_lin.shape[1] // log_decay.shape[0]
    lin_out = lightning_heads(q_lin, k_lin, v_lin, log_decay)
    soft_out = softmax_heads(q_soft, k_soft, v_soft, head_width)
    lin_term = jnp.dot(lin_out, wo_lin, preferred_element_type=jnp.float32)
    soft_term = jnp.dot(soft_out, wo_soft, preferred_element_type=jnp.float32)
    lin_sum, soft_sum = (
        lax.psum_scatter(
            lin_term.astype(jnp.bfloat16).astype(jnp.float32).astype(jnp.bfloat16),
            "head",
            scatter_dimension=1,
            tiled=True,
        ).astype(jnp.float32),
        lax.psum_scatter(
            soft_term.astype(jnp.bfloat16).astype(jnp.float32).astype(jnp.bfloat16),
            "head",
            scatter_dimension=1,
            tiled=True,
        ).astype(jnp.float32),
    )
    return (lin_sum.astype(jnp.bfloat16), soft_sum.astype(jnp.bfloat16))


def solution(mesh):
    in_specs = (
        P("seq", "head"),
        P("seq", "head"),
        P("seq", "head"),
        P("head", "seq"),
        P("seq", "head"),
        P("seq", "head"),
        P("seq", "head"),
        P("head", None),
        P("head", None),
    )
    out_specs = (P("seq", "head"), P("seq", "head"))
    return jax.shard_map(local, mesh=mesh, in_specs=in_specs, out_specs=out_specs, check_vma=False)
```

profile of v0, /device:TPU:0, one launch (start us, length us, event | category | flops | bytes accessed | tf_op | source)
XLA Modules:
  0.0 389.1 jit_solution(17133437121583700277)
XLA Ops:
  9.3 1.0 copy.69
  10.4 1.8 convolution_convert_fusion.2
  13.8 1.2 dynamic-slice
  15.9 43.7 %all-reduce = bf16[32]{0:T(256)(128)(2,1)S(1)} all-reduce(bf16[32]{0:T(256)(128)(2,1)S(1)} %dynamic-update-slice), channel_id=2, replica_groups=mesh['seq'=16,'head'=2] {'seq'}, use_global_device_ids=true, to_apply=%add | all-reduce | flops 32 | bytes 128
  60.7 1.1 convolution_multiply_fusion.4
  61.8 8.6 %all-gather.10.cloned.1.call-done = bf16[32,128,128]{2,1,0:T(8,128)(2,1)} async-done(((bf16[2,128,128]{2,1,0:T(8,128)(2,1)}), bf16[32,128,128]{2,1,0:T(8,128)(2,1)}) %all-gather.10.cloned.1.call-update) | async-done | bytes 1048592 | tf_op jit(solution)/shard_map/all_gather | solution.py:14
  70.5 15.6 %while.39 = (s32[]{:T(128)}, f32[2,128,128]{2,1,0:T(8,128)S(1)}, s32[]{:T(128)}, bf16[16,2]{1,0:T(8,128)(2,1)S(1)}, bf16[16,2,128,128]{3,2,1,0:T(8,128)(2,1)}, /*index=5*/s32[]{:T(128)}, s32[]{:T(128)}) while((s32[]{:T(128)}, f32[2,128,128]{2,1,0:T(8,128)S(1)}, s32[]{:T(128)}, bf16[16,2]{1,0:T(8,128)(2,1)S(1)}, ...), condition=%wide.region_3.4_spmd.clone, body=%wide.region_2.3_spmd.clone.sunk | while | flops 163846 | bytes 327813 | solution.py:31
  86.9 2.1 convolution_convert_fusion.1
  89.1 43.7 %all-gather.6.cloned.1.call-done = bf16[4096,256]{1,0:T(8,128)(2,1)} async-done(((bf16[256,256]{1,0:T(8,128)(2,1)}), bf16[4096,256]{1,0:T(8,128)(2,1)}) %all-gather.6.cloned.1.call-update) | async-done | bytes 2097168 | tf_op jit(solution)/shard_map/all_gather | solution.py:132
  132.8 4.0 %reshape.143 = bf16[32,128,2,128]{3,2,1,0:T(2,128)(2,1)} reshape(bf16[4096,256]{1,0:T(8,128)(2,1)} %all-gather.6.cloned.1.call-done) | data formatting | bytes 4194304 | tf_op jit(solution)/shard_map/reshape | solution.py:136
  136.8 58.2 %all-gather.8.cloned.1.call-done = bf16[4096,256]{1,0:T(8,128)(2,1)} async-done(((bf16[256,256]{1,0:T(8,128)(2,1)}), bf16[4096,256]{1,0:T(8,128)(2,1)}) %all-gather.8.cloned.1.call-update) | async-done | bytes 2097168 | tf_op jit(solution)/shard_map/all_gather | solution.py:133
  195.0 4.0 %reshape.144 = bf16[32,128,2,128]{3,2,1,0:T(2,128)(2,1)} reshape(bf16[4096,256]{1,0:T(8,128)(2,1)} %all-gather.8.cloned.1.call-done) | data formatting | bytes 4194304 | tf_op jit(solution)/shard_map/reshape | solution.py:137
  199.0 141.2 %while.38 = (s32[]{:T(128)}, f32[2,128]{1,0:T(2,128)S(1)}, f32[2,128]{1,0:T(2,128)S(1)}, f32[128,2,128]{2,0,1:T(8,128)S(1)}, f32[2,128]{1,0:T(2,128)S(1)}, /*ind...) while((s32[]{:T(128)}, f32[2,128]{1,0:T(2,128)S(1)}, ...), condition=%wide.region_23.24_spmd.clone.clone, body=%wide.region_6.23_spmd.clone.clone.sunk | while | flops 34162200 | bytes 2311003 | solution.py:150
  202.3 1.0 constant_dynamic-slice_fusion.3
  207.7 1.0 constant_dynamic-slice_fusion.3
  212.6 1.0 constant_dynamic-slice_fusion.3
  216.9 1.0 constant_dynamic-slice_fusion.3
  221.3 1.0 constant_dynamic-slice_fusion.3
  225.7 1.0 constant_dynamic-slice_fusion.3
  230.0 1.0 constant_dynamic-slice_fusion.3
  234.4 1.0 constant_dynamic-slice_fusion.3
  238.7 1.0 constant_dynamic-slice_fusion.3
  243.1 1.0 constant_dynamic-slice_fusion.3
  247.5 1.0 constant_dynamic-slice_fusion.3
  251.8 1.0 constant_dynamic-slice_fusion.3
  256.2 1.0 constant_dynamic-slice_fusion.3
  260.5 1.0 constant_dynamic-slice_fusion.3
  264.9 1.0 constant_dynamic-slice_fusion.3
  269.3 1.0 constant_dynamic-slice_fusion.3
  273.6 1.0 constant_dynamic-slice_fusion.3
  340.4 3.6 convolution_convert_fusion
  344.1 38.5 %reduce-scatter.5.cloned.1.call-done = bf16[256,2048]{1,0:T(8,128)(2,1)} async-done(((bf16[256,4096]{1,0:T(8,128)(2,1)}), bf16[256,2048]{1,0:T(8,128)(2,1)}) %reduce-scatter.5.cloned.1.call-update) | async-done | bytes 1048592 | tf_op jit(solution)/shard_map/reduce_scatter | solution.py:173
  (369 shorter events, 63.6 us)
Async XLA Ops:
  7.2 79.8 %copy-start = (bf16[256,4096]{1,0:T(8,128)(2,1)S(1)}, bf16[256,4096]{1,0:T(8,128)(2,1)}, u32[]{:S(2)}) copy-start(bf16[256,4096]{1,0:T(8,128)(2,1)} %param.28) | copy-start | bytes 6291460
  7.2 63.3 %all-gather.10.cloned.1.call-start = ((), (), s32[]{:S(2)}) async-start(), calls=%async_computation.6 | async-start | bytes 1114112 | tf_op jit(solution)/shard_map/all_gather | solution.py:14
  10.3 75.7 %copy-start.2 = (bf16[256,256]{1,0:T(8,128)(2,1)S(1)}, bf16[256,256]{1,0:T(8,128)(2,1)}, u32[]{:S(2)}) copy-start(bf16[256,256]{1,0:T(8,128)(2,1)} %param.21) | copy-start | bytes 393220
  12.2 120.6 %all-gather.6.cloned.1.call-start = ((), (), s32[]{:S(2)}) async-start(), calls=%async_computation.3 | async-start | bytes 2228224 | tf_op jit(solution)/shard_map/all_gather | solution.py:132
  13.0 73.4 %copy-start.1 = (bf16[256,256]{1,0:T(8,128)(2,1)S(1)}, bf16[256,256]{1,0:T(8,128)(2,1)}, u32[]{:S(2)}) copy-start(bf16[256,256]{1,0:T(8,128)(2,1)} %param.23) | copy-start | bytes 393220
  13.0 182.0 %all-gather.8.cloned.1.call-start = ((), (), s32[]{:S(2)}) async-start(), calls=%async_computation.4 | async-start | bytes 2228224 | tf_op jit(solution)/shard_map/all_gather | solution.py:133
  13.7 330.4 %reduce-scatter.3.cloned.1.call-start = ((), (), s32[]{:S(2)}) async-start(), calls=%async_computation.2 | async-start | bytes 3145728 | tf_op jit(solution)/shard_map/reduce_scatter | solution.py:167
  89.0 293.5 %reduce-scatter.5.cloned.1.call-start = ((), (), s32[]{:S(2)}) async-start(), calls=%async_computation.5 | async-start | bytes 3145728 | tf_op jit(solution)/shard_map/reduce_scatter | solution.py:173
Sparse Core Ops, SparseCore 0:
  12.3 58.0 all-gather.9
  73.2 59.5 all-gather.5
  135.6 59.3 all-gather.7
  197.6 8.2 reduce-scatter.2
  344.2 38.3 reduce-scatter.4
where the time goes:
time: 393 us; the launch traced here: 389 us
  waiting for transfers between devices  150 us (38%)
  loops' own time  89.1 us (23%)
  local copies, waits for them, and re-layouts  63.5 us (16%)
  blocking collectives  43.7 us (11%)
  other arithmetic  16.9 us (4%)
  between operations  14.6 us (4%)
  matrix products  10.7 us (3%)
    another operation x1, loops' own time, softmax_heads(): carry, _ = lax.scan(inner, carry, (key_blocks, value_blocks, firsts))  85.6 us
    all_gather x1, waiting for transfers between devices, softmax_heads(): value_piece = lax.all_gather(v_soft, 'seq', axis=0, tiled=True)  58.2 us
    dynamic_slice x128, local copies, waits for them, and re-layouts, softmax_heads(): carry, _ = lax.scan(inner, carry, (key_blocks, value_blocks, firsts))  50.6 us
    all_gather x1, waiting for transfers between devices, softmax_heads(): key_piece = lax.all_gather(k_soft, 'seq', axis=0, tiled=True)  43.7 us
    unnamed x1, blocking collectives  43.7 us
    reduce_scatter x1, waiting for transfers between devices, local(): lax.psum_scatter(soft_term.astype(jnp.bfloat16).astype(jnp.float32).astyp...  38.5 us
    select_n x16, other arithmetic, turn(): return jax.tree.map(lambda a, b: jnp.where(reached, a, b), new, before)  14.9 us
    all_gather x1, waiting for transfers between devices, prefix(): lax.all_gather(part.astype(kind), axis)  8.65 us
  transfers between devices with their start and end apart: 5, of which 4 were waited for; matrix products, arithmetic and copies ran while one was open for 22% of the time, Pallas kernels for 0%

commit v1 on v0

--- a/solution.py
+++ b/solution.py
@@ -6,6 +6,23 @@
 
 HIGHEST = lax.Precision.HIGHEST
 NEG_BIG = -1e30
+
+
+def laid_out(blocks, dim):
+    blocks = jnp.moveaxis(blocks, 0, dim)
+    lengths = blocks.shape
+    return blocks.reshape(*lengths[:dim], lengths[dim] * lengths[dim + 1], *lengths[dim + 2 :])
+
+
+def gather_around(x, axis, dim):
+    peers = lax.axis_size(axis)
+    right = [(i, (i + 1) % peers) for i in range(peers)]
+    tiles = [x]
+    while len(tiles) < peers:
+        tiles.append(lax.ppermute(tiles[-1], axis, right))
+    here = lax.axis_index(axis)
+    tiles = jnp.stack(tiles)[(here - jnp.arange(peers)) % peers]
+    return laid_out(tiles, dim)
 
 
 def prefix(shard, axis, combine, identity):
@@ -130,7 +147,7 @@
     )
     carry = start_state
     key_piece = lax.all_gather(k_soft, "seq", axis=0, tiled=True)
-    value_piece = lax.all_gather(v_soft, "seq", axis=0, tiled=True)
+    value_piece = gather_around(v_soft, "seq", 0)
     piece_rows = key_piece.shape[0]
     blocks = piece_rows // half_rows
     key_blocks = key_piece.reshape(blocks, half_rows, head_count, head_width)

time: 393 us -> 414 us (1.053)
  local copies, waits for them, and re-layouts: 63.5 us -> 77.2 us
  waiting for transfers between devices: 150 us -> 156 us
    ppermute x0 -> x15, waiting for transfers between devices: none -> 121 us  [gather_around(): tiles.append(lax.ppermute(tiles[-1], axis, right))]
    all_gather x1 -> x0, waiting for transfers between devices: 58.2 us -> none  [softmax_heads(): value_piece = lax.all_gather(v_soft, 'seq', axis=0, tiled=True)]
    all_gather x1, waiting for transfers between devices: 43.7 us -> 0.02 us  [softmax_heads(): key_piece = lax.all_gather(k_soft, 'seq', axis=0, tiled=True)]
    unnamed x12 -> x31, local copies, waits for them, and re-layouts: 1.61 us -> 11.9 us
    all_gather x1, waiting for transfers between devices: 8.65 us -> 0.01 us  [prefix(): lax.all_gather(part.astype(kind), axis)]
    another operation x6 -> x8, local copies, waits for them, and re-layouts: 0.03 us -> 4.68 us  [the longest x1 3.99 us: softmax_heads(): value_piece.reshape(blocks, half_rows, head_count, head_width)]
  transfers between devices with their start and end apart: 5 -> 19, of which waited for: 4 -> 15; matrix products, arithmetic and copies ran while one was open for 22% -> 24% of each run, Pallas kernels for 0% -> 0%
where the time goes in v1:
time: 414 us; the launch traced here: 410 us
  waiting for transfers between devices  156 us (38%)
  loops' own time  89 us (21%)
  local copies, waits for them, and re-layouts  77.2 us (19%)
  blocking collectives  41.6 us (10%)
  other arithmetic  16.9 us (4%)
  between operations  14.7 us (4%)
  matrix products  10.7 us (3%)
    ppermute x15, waiting for transfers between devices, gather_around(): tiles.append(lax.ppermute(tiles[-1], axis, right))  121 us
    another operation x1, loops' own time, softmax_heads(): carry, _ = lax.scan(inner, carry, (key_blocks, value_blocks, firsts))  85.7 us
    dynamic_slice x128, local copies, waits for them, and re-layouts, softmax_heads(): carry, _ = lax.scan(inner, carry, (key_blocks, value_blocks, firsts))  50.6 us
    unnamed x1, blocking collectives  41.6 us
    reduce_scatter x1, waiting for transfers between devices, local(): lax.psum_scatter(soft_term.astype(jnp.bfloat16).astype(jnp.float32).astyp...  35.3 us
    select_n x16, other arithmetic, turn(): return jax.tree.map(lambda a, b: jnp.where(reached, a, b), new, before)  14.9 us
    unnamed x31, local copies, waits for them, and re-layouts  11.9 us
  transfers between devices with their start and end apart: 19, of which 15 were waited for; matrix products, arithmetic and copies ran while one was open for 24% of the time, Pallas kernels for 0%

profile of v1, /device:TPU:0, one launch (start us, length us, event | category | flops | bytes accessed | tf_op | source)
XLA Modules:
  0.0 409.8 jit_solution(17242743665083099985)
XLA Ops:
  9.4 1.0 copy.69
  10.4 1.8 convolution_convert_fusion.2
  12.3 3.0 collective-permute-start
  15.3 1.6 bitcast_dynamic-update-slice_fusion.15
  16.9 1.1 convolution_multiply_fusion.4
  19.7 41.6 %all-reduce = bf16[32]{0:T(256)(128)(2,1)S(1)} all-reduce(bf16[32]{0:T(256)(128)(2,1)S(1)} %dynamic-update-slice), channel_id=2, replica_groups=mesh['seq'=16,'head'=2] {'seq'}, use_global_device_ids=true, to_apply=%add | all-reduce | flops 32 | bytes 128
  62.1 10.0 %collective-permute-done.1 = bf16[256,256]{1,0:T(8,128)(2,1)S(1)} collective-permute-done((bf16[256,256]{1,0:T(8,128)(2,1)S(1)}, bf16[256,256]{1,0:T(8,128)(2,1)S(1)}, u32[]{:S(2)}, u32[]{:S(2)}) %collective-permute-start.1) | collective-permute-done | bytes 131104 | tf_op jit(solution)/shard_map/ppermute | solution.py:22
  72.8 7.9 %collective-permute-done.2 = bf16[256,256]{1,0:T(8,128)(2,1)S(1)} collective-permute-done((bf16[256,256]{1,0:T(8,128)(2,1)S(1)}, bf16[256,256]{1,0:T(8,128)(2,1)S(1)}, u32[]{:S(2)}, u32[]{:S(2)}) %collective-permute-start.2) | collective-permute-done | bytes 131104 | tf_op jit(solution)/shard_map/ppermute | solution.py:22
  81.3 8.0 %collective-permute-done.3 = bf16[256,256]{1,0:T(8,128)(2,1)S(1)} collective-permute-done((bf16[256,256]{1,0:T(8,128)(2,1)S(1)}, bf16[256,256]{1,0:T(8,128)(2,1)S(1)}, u32[]{:S(2)}, u32[]{:S(2)}) %collective-permute-start.3) | collective-permute-done | bytes 131104 | tf_op jit(solution)/shard_map/ppermute | solution.py:22
  90.0 8.3 %collective-permute-done.4 = bf16[256,256]{1,0:T(8,128)(2,1)S(1)} collective-permute-done((bf16[256,256]{1,0:T(8,128)(2,1)S(1)}, bf16[256,256]{1,0:T(8,128)(2,1)S(1)}, u32[]{:S(2)}, u32[]{:S(2)}) %collective-permute-start.4) | collective-permute-done | bytes 131104 | tf_op jit(solution)/shard_map/ppermute | solution.py:22
  99.0 9.7 %collective-permute-done.5 = bf16[256,256]{1,0:T(8,128)(2,1)S(1)} collective-permute-done((bf16[256,256]{1,0:T(8,128)(2,1)S(1)}, bf16[256,256]{1,0:T(8,128)(2,1)S(1)}, u32[]{:S(2)}, u32[]{:S(2)}) %collective-permute-start.5) | collective-permute-done | bytes 131104 | tf_op jit(solution)/shard_map/ppermute | solution.py:22
  109.4 8.1 %collective-permute-done.6 = bf16[256,256]{1,0:T(8,128)(2,1)S(1)} collective-permute-done((bf16[256,256]{1,0:T(8,128)(2,1)S(1)}, bf16[256,256]{1,0:T(8,128)(2,1)S(1)}, u32[]{:S(2)}, u32[]{:S(2)}) %collective-permute-start.6) | collective-permute-done | bytes 131104 | tf_op jit(solution)/shard_map/ppermute | solution.py:22
  118.2 10.9 %collective-permute-done.7 = bf16[256,256]{1,0:T(8,128)(2,1)S(1)} collective-permute-done((bf16[256,256]{1,0:T(8,128)(2,1)S(1)}, bf16[256,256]{1,0:T(8,128)(2,1)S(1)}, u32[]{:S(2)}, u32[]{:S(2)}) %collective-permute-start.7) | collective-permute-done | bytes 131104 | tf_op jit(solution)/shard_map/ppermute | solution.py:22
  129.8 10.6 %collective-permute-done.8 = bf16[256,256]{1,0:T(8,128)(2,1)S(1)} collective-permute-done((bf16[256,256]{1,0:T(8,128)(2,1)S(1)}, bf16[256,256]{1,0:T(8,128)(2,1)S(1)}, u32[]{:S(2)}, u32[]{:S(2)}) %collective-permute-start.8) | collective-permute-done | bytes 131104 | tf_op jit(solution)/shard_map/ppermute | solution.py:22
  141.1 7.9 %collective-permute-done.9 = bf16[256,256]{1,0:T(8,128)(2,1)S(1)} collective-permute-done((bf16[256,256]{1,0:T(8,128)(2,1)S(1)}, bf16[256,256]{1,0:T(8,128)(2,1)S(1)}, u32[]{:S(2)}, u32[]{:S(2)}) %collective-permute-start.9) | collective-permute-done | bytes 131104 | tf_op jit(solution)/shard_map/ppermute | solution.py:22
  149.7 7.9 %collective-permute-done.10 = bf16[256,256]{1,0:T(8,128)(2,1)S(1)} collective-permute-done((bf16[256,256]{1,0:T(8,128)(2,1)S(1)}, bf16[256,256]{1,0:T(8,128)(2,1)S(1)}, u32[]{:S(2)}, u32[]{:S(2)}) %collective-permute-start.10) | collective-permute-done | bytes 131104 | tf_op jit(solution)/shard_map/ppermute | solution.py:22
  158.2 7.9 %collective-permute-done.11 = bf16[256,256]{1,0:T(8,128)(2,1)S(1)} collective-permute-done((bf16[256,256]{1,0:T(8,128)(2,1)S(1)}, bf16[256,256]{1,0:T(8,128)(2,1)S(1)}, u32[]{:S(2)}, u32[]{:S(2)}) %collective-permute-start.11) | collective-permute-done | bytes 131104 | tf_op jit(solution)/shard_map/ppermute | solution.py:22
  166.8 7.9 %collective-permute-done.12 = bf16[256,256]{1,0:T(8,128)(2,1)S(1)} collective-permute-done((bf16[256,256]{1,0:T(8,128)(2,1)S(1)}, bf16[256,256]{1,0:T(8,128)(2,1)S(1)}, u32[]{:S(2)}, u32[]{:S(2)}) %collective-permute-start.12) | collective-permute-done | bytes 131104 | tf_op jit(solution)/shard_map/ppermute | solution.py:22
  175.3 7.9 %collective-permute-done.13 = bf16[256,256]{1,0:T(8,128)(2,1)S(1)} collective-permute-done((bf16[256,256]{1,0:T(8,128)(2,1)S(1)}, bf16[256,256]{1,0:T(8,128)(2,1)S(1)}, u32[]{:S(2)}, u32[]{:S(2)}) %collective-permute-start.13) | collective-permute-done | bytes 131104 | tf_op jit(solution)/shard_map/ppermute | solution.py:22
  183.9 7.9 %collective-permute-done.14 = bf16[256,256]{1,0:T(8,128)(2,1)S(1)} collective-permute-done((bf16[256,256]{1,0:T(8,128)(2,1)S(1)}, bf16[256,256]{1,0:T(8,128)(2,1)S(1)}, u32[]{:S(2)}, u32[]{:S(2)}) %collective-permute-start.14) | collective-permute-done | bytes 131104 | tf_op jit(solution)/shard_map/ppermute | solution.py:22
  192.5 3.6 gather_fusion
  196.1 4.0 reshape.197
  200.1 15.6 %while.39 = (s32[]{:T(128)}, f32[2,128,128]{2,1,0:T(8,128)S(1)}, s32[]{:T(128)}, bf16[16,2]{1,0:T(8,128)(2,1)S(1)}, bf16[16,2,128,128]{3,2,1,0:T(8,128)(2,1)}, /*index=5*/s32[]{:T(128)}, s32[]{:T(128)}) while((s32[]{:T(128)}, f32[2,128,128]{2,1,0:T(8,128)S(1)}, s32[]{:T(128)}, bf16[16,2]{1,0:T(8,128)(2,1)S(1)}, ...), condition=%wide.region_3.4_spmd.clone, body=%wide.region_2.3_spmd.clone.sunk | while | flops 163846 | bytes 327805 | solution.py:48
  216.5 2.0 convolution_convert_fusion.1
  218.7 4.0 reshape.196
  222.8 141.1 %while.38 = (s32[]{:T(128)}, f32[2,128]{1,0:T(2,128)S(1)}, f32[2,128]{1,0:T(2,128)S(1)}, f32[128,2,128]{2,0,1:T(8,128)S(1)}, f32[2,128]{1,0:T(2,128)S(1)}, /*ind...) while((s32[]{:T(128)}, f32[2,128]{1,0:T(2,128)S(1)}, ...), condition=%wide.region_23.24_spmd.clone.clone, body=%wide.region_6.23_spmd.clone.clone.sunk | while | flops 34162200 | bytes 2310995 | solution.py:167
  226.0 1.0 constant_dynamic-slice_fusion.3
  231.4 1.0 constant_dynamic-slice_fusion.3
  236.3 1.0 constant_dynamic-slice_fusion.3
  240.6 1.0 constant_dynamic-slice_fusion.3
  364.2 3.7 convolution_convert_fusion
  367.9 35.3 %reduce-scatter.5.cloned.1.call-done = bf16[256,2048]{1,0:T(8,128)(2,1)} async-done(((bf16[256,4096]{1,0:T(8,128)(2,1)}), bf16[256,2048]{1,0:T(8,128)(2,1)}) %reduce-scatter.5.cloned.1.call-update) | async-done | bytes 1048592 | tf_op jit(solution)/shard_map/reduce_scatter | solution.py:190
  (419 shorter events, 84.5 us)
Async XLA Ops:
  7.2 209.4 %copy-start = (bf16[256,4096]{1,0:T(8,128)(2,1)S(1)}, bf16[256,4096]{1,0:T(8,128)(2,1)}, u32[]{:S(2)}) copy-start(bf16[256,4096]{1,0:T(8,128)(2,1)} %param.28) | copy-start | bytes 6291460
  7.2 11.0 %copy-start.4 = (u32[32]{0:T(128)S(1)}, u32[32]{0:T(128)}, u32[]{:S(2)}) copy-start(u32[32]{0:T(128)} %constant.137) | copy-start | bytes 388
  7.2 10.9 %copy-start.2 = (bf16[256,256]{1,0:T(8,128)(2,1)S(1)}, bf16[256,256]{1,0:T(8,128)(2,1)}, u32[]{:S(2)}) copy-start(bf16[256,256]{1,0:T(8,128)(2,1)} %param.25) | copy-start | bytes 393220
  7.2 192.9 %all-gather.7.cloned.1.call-start = ((), (), s32[]{:S(2)}) async-start(), calls=%async_computation.5 | async-start | bytes 1114112 | tf_op jit(solution)/shard_map/all_gather | solution.py:31
  12.2 206.4 %all-gather.5.cloned.1.call-start = ((), (), s32[]{:S(2)}) async-start(), calls=%async_computation.3 | async-start | bytes 2228224 | tf_op jit(solution)/shard_map/all_gather | solution.py:149
  12.3 49.1 %collective-permute-start = (bf16[256,256]{1,0:T(8,128)(2,1)}, bf16[256,256]{1,0:T(8,128)(2,1)S(1)}, u32[]{:S(2)}, u32[]{:S(2)}) collective-permute-start(bf16[256,256]{1,0:T(8,128)(2,1)} %param.27), channel_id=1, source_target_pairs={{0,2},{2,4},{4,6},{6,8},{8,10},{10,12},{12,14},{14,16},{16,18},{18... | collective-permute-start | bytes 393224 | tf_op jit(solution)/shard_map/ppermute | solution.py:22
  15.3 352.6 %reduce-scatter.3.cloned.1.call-start = ((), (), s32[]{:S(2)}) async-start(), calls=%async_computation.2 | async-start | bytes 3145728 | tf_op jit(solution)/shard_map/reduce_scatter | solution.py:184
  61.4 10.7 %collective-permute-start.1 = (bf16[256,256]{1,0:T(8,128)(2,1)S(1)}, bf16[256,256]{1,0:T(8,128)(2,1)S(1)}, u32[]{:S(2)}, u32[]{:S(2)}) collective-permute-start(bf16[256,256]{1,0:T(8,128)(2,1)S(1)} %collective-permute-done), channel_id=1, source_target_pairs={{0,2},{2,4},{4,6},{6,8},{8,10},{10,12},{12,14},{14,16},{16,18},{18... | collective-permute-start | bytes 393224 | tf_op jit(solution)/shard_map/ppermute | solution.py:22
  72.1 8.6 %collective-permute-start.2 = (bf16[256,256]{1,0:T(8,128)(2,1)S(1)}, bf16[256,256]{1,0:T(8,128)(2,1)S(1)}, u32[]{:S(2)}, u32[]{:S(2)}) collective-permute-start(bf16[256,256]{1,0:T(8,128)(2,1)S(1)} %collective-permute-done.1), channel_id=1, source_target_pairs={{0,2},{2,4},{4,6},{6,8},{8,10},{10,12},{12,14},{14,16},{16,18},{18... | collective-permute-start | bytes 393224 | tf_op jit(solution)/shard_map/ppermute | solution.py:22
  80.7 8.7 %collective-permute-start.3 = (bf16[256,256]{1,0:T(8,128)(2,1)S(1)}, bf16[256,256]{1,0:T(8,128)(2,1)S(1)}, u32[]{:S(2)}, u32[]{:S(2)}) collective-permute-start(bf16[256,256]{1,0:T(8,128)(2,1)S(1)} %collective-permute-done.2), channel_id=1, source_target_pairs={{0,2},{2,4},{4,6},{6,8},{8,10},{10,12},{12,14},{14,16},{16,18},{18... | collective-permute-start | bytes 393224 | tf_op jit(solution)/shard_map/ppermute | solution.py:22
  89.4 9.0 %collective-permute-start.4 = (bf16[256,256]{1,0:T(8,128)(2,1)S(1)}, bf16[256,256]{1,0:T(8,128)(2,1)S(1)}, u32[]{:S(2)}, u32[]{:S(2)}) collective-permute-start(bf16[256,256]{1,0:T(8,128)(2,1)S(1)} %collective-permute-done.3), channel_id=1, source_target_pairs={{0,2},{2,4},{4,6},{6,8},{8,10},{10,12},{12,14},{14,16},{16,18},{18... | collective-permute-start | bytes 393224 | tf_op jit(solution)/shard_map/ppermute | solution.py:22
  98.3 10.4 %collective-permute-start.5 = (bf16[256,256]{1,0:T(8,128)(2,1)S(1)}, bf16[256,256]{1,0:T(8,128)(2,1)S(1)}, u32[]{:S(2)}, u32[]{:S(2)}) collective-permute-start(bf16[256,256]{1,0:T(8,128)(2,1)S(1)} %collective-permute-done.4), channel_id=1, source_target_pairs={{0,2},{2,4},{4,6},{6,8},{8,10},{10,12},{12,14},{14,16},{16,18},{18... | collective-permute-start | bytes 393224 | tf_op jit(solution)/shard_map/ppermute | solution.py:22
  108.7 8.8 %collective-permute-start.6 = (bf16[256,256]{1,0:T(8,128)(2,1)S(1)}, bf16[256,256]{1,0:T(8,128)(2,1)S(1)}, u32[]{:S(2)}, u32[]{:S(2)}) collective-permute-start(bf16[256,256]{1,0:T(8,128)(2,1)S(1)} %collective-permute-done.5), channel_id=1, source_target_pairs={{0,2},{2,4},{4,6},{6,8},{8,10},{10,12},{12,14},{14,16},{16,18},{18... | collective-permute-start | bytes 393224 | tf_op jit(solution)/shard_map/ppermute | solution.py:22
  117.5 11.6 %collective-permute-start.7 = (bf16[256,256]{1,0:T(8,128)(2,1)S(1)}, bf16[256,256]{1,0:T(8,128)(2,1)S(1)}, u32[]{:S(2)}, u32[]{:S(2)}) collective-permute-start(bf16[256,256]{1,0:T(8,128)(2,1)S(1)} %collective-permute-done.6), channel_id=1, source_target_pairs={{0,2},{2,4},{4,6},{6,8},{8,10},{10,12},{12,14},{14,16},{16,18},{18... | collective-permute-start | bytes 393224 | tf_op jit(solution)/shard_map/ppermute | solution.py:22
  129.1 11.3 %collective-permute-start.8 = (bf16[256,256]{1,0:T(8,128)(2,1)S(1)}, bf16[256,256]{1,0:T(8,128)(2,1)S(1)}, u32[]{:S(2)}, u32[]{:S(2)}) collective-permute-start(bf16[256,256]{1,0:T(8,128)(2,1)S(1)} %collective-permute-done.7), channel_id=1, source_target_pairs={{0,2},{2,4},{4,6},{6,8},{8,10},{10,12},{12,14},{14,16},{16,18},{18... | collective-permute-start | bytes 393224 | tf_op jit(solution)/shard_map/ppermute | solution.py:22
  140.4 8.6 %collective-permute-start.9 = (bf16[256,256]{1,0:T(8,128)(2,1)S(1)}, bf16[256,256]{1,0:T(8,128)(2,1)S(1)}, u32[]{:S(2)}, u32[]{:S(2)}) collective-permute-start(bf16[256,256]{1,0:T(8,128)(2,1)S(1)} %collective-permute-done.8), channel_id=1, source_target_pairs={{0,2},{2,4},{4,6},{6,8},{8,10},{10,12},{12,14},{14,16},{16,18},{18... | collective-permute-start | bytes 393224 | tf_op jit(solution)/shard_map/ppermute | solution.py:22
  149.0 8.6 %collective-permute-start.10 = (bf16[256,256]{1,0:T(8,128)(2,1)S(1)}, bf16[256,256]{1,0:T(8,128)(2,1)S(1)}, u32[]{:S(2)}, u32[]{:S(2)}) collective-permute-start(bf16[256,256]{1,0:T(8,128)(2,1)S(1)} %collective-permute-done.9), channel_id=1, source_target_pairs={{0,2},{2,4},{4,6},{6,8},{8,10},{10,12},{12,14},{14,16},{16,18},{18... | collective-permute-start | bytes 393224 | tf_op jit(solution)/shard_map/ppermute | solution.py:22
  157.5 8.6 %collective-permute-start.11 = (bf16[256,256]{1,0:T(8,128)(2,1)S(1)}, bf16[256,256]{1,0:T(8,128)(2,1)S(1)}, u32[]{:S(2)}, u32[]{:S(2)}) collective-permute-start(bf16[256,256]{1,0:T(8,128)(2,1)S(1)} %collective-permute-done.10), channel_id=1, source_target_pairs={{0,2},{2,4},{4,6},{6,8},{8,10},{10,12},{12,14},{14,16},{16,18},{18... | collective-permute-start | bytes 393224 | tf_op jit(solution)/shard_map/ppermute | solution.py:22
  166.1 8.6 %collective-permute-start.12 = (bf16[256,256]{1,0:T(8,128)(2,1)S(1)}, bf16[256,256]{1,0:T(8,128)(2,1)S(1)}, u32[]{:S(2)}, u32[]{:S(2)}) collective-permute-start(bf16[256,256]{1,0:T(8,128)(2,1)S(1)} %collective-permute-done.11), channel_id=1, source_target_pairs={{0,2},{2,4},{4,6},{6,8},{8,10},{10,12},{12,14},{14,16},{16,18},{18... | collective-permute-start | bytes 393224 | tf_op jit(solution)/shard_map/ppermute | solution.py:22
  174.7 8.6 %collective-permute-start.13 = (bf16[256,256]{1,0:T(8,128)(2,1)S(1)}, bf16[256,256]{1,0:T(8,128)(2,1)S(1)}, u32[]{:S(2)}, u32[]{:S(2)}) collective-permute-start(bf16[256,256]{1,0:T(8,128)(2,1)S(1)} %collective-permute-done.12), channel_id=1, source_target_pairs={{0,2},{2,4},{4,6},{6,8},{8,10},{10,12},{12,14},{14,16},{16,18},{18... | collective-permute-start | bytes 393224 | tf_op jit(solution)/shard_map/ppermute | solution.py:22
  183.2 8.6 %collective-permute-start.14 = (bf16[256,256]{1,0:T(8,128)(2,1)S(1)}, bf16[256,256]{1,0:T(8,128)(2,1)S(1)}, u32[]{:S(2)}, u32[]{:S(2)}) collective-permute-start(bf16[256,256]{1,0:T(8,128)(2,1)S(1)} %collective-permute-done.13), channel_id=1, source_target_pairs={{0,2},{2,4},{4,6},{6,8},{8,10},{10,12},{12,14},{14,16},{16,18},{18... | collective-permute-start | bytes 393224 | tf_op jit(solution)/shard_map/ppermute | solution.py:22
  196.1 19.6 %copy-start.3 = (bf16[256,256]{1,0:T(8,128)(2,1)S(1)}, bf16[256,256]{1,0:T(8,128)(2,1)}, u32[]{:S(2)}) copy-start(bf16[256,256]{1,0:T(8,128)(2,1)} %param.21) | copy-start | bytes 393220
  200.1 15.9 %copy-start.1 = (bf16[256,256]{1,0:T(8,128)(2,1)S(1)}, bf16[256,256]{1,0:T(8,128)(2,1)}, u32[]{:S(2)}) copy-start(bf16[256,256]{1,0:T(8,128)(2,1)} %param.23) | copy-start | bytes 393220
  218.6 184.6 %reduce-scatter.5.cloned.1.call-start = ((), (), s32[]{:S(2)}) async-start(), calls=%async_computation.4 | async-start | bytes 3145728 | tf_op jit(solution)/shard_map/reduce_scatter | solution.py:190
Sparse Core Ops, SparseCore 0:
  12.3 60.3 all-gather.6
  75.5 65.1 all-gather.4
  218.7 5.4 reduce-scatter.2
  368.0 35.1 reduce-scatter.4
